TPU v7x, 512 devices: a whole 4x4x16 slice. The times are simulated.
512 devices in a mesh: tm: 32 (over x, y, core), group: 16 (over z).
Axes of the slice: x: 4, y: 4, z: 16, core: 2. Of those that a mesh axis runs over, the one named last changes fastest.
Arguments:
- propagators: float32 [32, 384, 384], P('tm'), may hold values from -1 to 1, as said below
- perturbation: float32 [32, 384, 384], P('tm', 'group'), as said below
Outputs:
- gradient: float32 [384, 384], P('tm')
Inputs may be any that keep to these rules, and one draw needn't show every extreme that they name: `propagators`: each slice's matrix is orthogonal. `perturbation`: each slice's matrix is symmetric.
All inputs are finite; a program needn't handle non-finite values.
Results may differ from a plain program's by a relative error of at most 0.00028.
Values sent between devices are 32-bit elements; how exact they have to be, the bound alone decides.
A program may use at most 128 MiB of HBM per device.

v0:
```python
import jax
import jax.numpy as jnp
from jax import lax
from jax.sharding import Mesh
from jax.sharding import PartitionSpec as P

TM = ("tm_0", "tm_1", "tm_2")


def nothing_yet(value, identity):
    return jnp.broadcast_to(jnp.asarray(identity, value.dtype), value.shape)


def entering(value, axes, combine, identity):
    before = start = nothing_yet(value, identity)
    subtotal = value
    for axis in reversed(axes):
        peers, place = (lax.axis_size(axis), lax.axis_index(axis))
        pieces = lax.all_gather(subtotal, axis)
        inside, subtotal = (start, start)
        for k in range(peers):
            passed = k < place
            subtotal = combine(subtotal, pieces[k])
            inside = jnp.where(passed, subtotal, inside)
        before = combine(inside, before)
    return before


def in_blocks(value, dim, peers):
    before, after = (value.shape[:dim], value.shape[dim + 1 :])
    return jnp.moveaxis(value.reshape(*before, peers, -1, *after), dim, 0)


def summed_on_arrival(value, axis, dim):
    parts = in_blocks(value, dim, lax.axis_size(axis))
    arrived = lax.all_to_all(parts, axis, split_axis=0, concat_axis=0, tiled=True)
    return arrived.sum(axis=0)


def total_of_pieces(value, axis):
    return lax.all_gather(value, axis).sum(0)


def times_high(left, right):
    return jnp.dot(left, right, precision=lax.Precision.HIGHEST, preferred_element_type=jnp.float32)


def compose(earlier, later):
    return times_high(later, earlier)


def body(propagators, perturbation):
    slice_count = propagators.shape[0]
    order_dim = propagators.shape[1]
    block_rows = perturbation.shape[1]
    identity = jnp.eye(order_dim, dtype=jnp.float32)
    local_prefixes = [identity]
    device_total = times_high(propagators[slice_count - 1], local_prefixes[-1])
    before = entering(device_total, TM, compose, identity)
    first_block = lax.axis_index("group") * block_rows
    prefix_rows = lax.dynamic_slice_in_dim(before, first_block, block_rows, 0)
    pulled = times_high(perturbation[0], before)
    conjugated = times_high(prefix_rows.T, pulled)
    row_sums = summed_on_arrival(conjugated, TM, 0)
    return total_of_pieces(row_sums, "group")


def solution(mesh):
    split = Mesh(
        mesh.devices.reshape(4, 4, 2, mesh.shape["group"]), ("tm_0", "tm_1", "tm_2", "group")
    )
    return jax.shard_map(
        body,
        mesh=split,
        in_specs=(P(TM, None, None), P(TM, "group", None)),
        out_specs=P(TM, None),
        check_vma=False,
    )
```

profile of v0, /device:TPU:8, one launch (start us, length us, event | category | flops | bytes accessed | tf_op | source)
XLA Modules:
  0.0 197.4 jit_solution(1742449011949335847)
XLA Ops:
  6.5 1.1 copy-done
  7.6 1.6 convolution_bitcast_fusion
  9.2 0.0 all-gather.9.cloned.1.call-update
  9.2 0.0 all-gather.11.cloned.1.call-start
  9.3 24.3 %all-gather.9.cloned.1.call-done = f32[768,384]{0,1:T(8,128)} async-done(((f32[384,384]{0,1:T(8,128)}), f32[768,384]{0,1:T(8,128)}) %all-gather.9.cloned.1.call-update) | async-done | bytes 1179664 | tf_op jit(solution)/shard_map/all_gather | solution.py:19
  33.5 1.8 fusion.25
  35.3 3.2 %fusion.27 = f32[384,384]{1,0:T(8,128)} fusion(f32[384,384]{1,0:T(8,128)S(1)} %fusion.25, f32[768,384]{0,1:T(8,128)} %all-gather.9.cloned.1.call-done), kind=kOutput, calls=%fused_computation.30 | convolution fusion | flops 679477248 | bytes 1769472 | tf_op jit(solution)/shard_map/dot_general | solution.py:45
  38.5 0.0 all-gather.11.cloned.1.call-update
  38.6 0.2 all-gather.13.cloned.1.call-start
  38.8 41.1 %all-gather.11.cloned.1.call-done = f32[1536,384]{1,0:T(8,128)} async-done(((f32[384,384]{1,0:T(8,128)}), f32[1536,384]{1,0:T(8,128)}) %all-gather.11.cloned.1.call-update) | async-done | bytes 2359312 | tf_op jit(solution)/shard_map/all_gather | solution.py:19
  79.8 1.9 fusion.17
  81.7 2.5 %fusion.19 = f32[384,384]{1,0:T(8,128)S(1)} fusion(f32[384,384]{1,0:T(8,128)S(1)} %fusion.17, f32[1536,384]{1,0:T(8,128)} %all-gather.11.cloned.1.call-done), kind=kOutput, calls=%fused_computation.22 | convolution fusion | flops 679477248 | bytes 1769472 | tf_op jit(solution)/shard_map/dot_general | solution.py:45
  84.3 1.3 fusion.21
  85.6 2.1 %fusion.23 = f32[384,384]{1,0:T(8,128)} fusion(f32[384,384]{1,0:T(8,128)S(1)} %fusion.21, f32[1536,384]{1,0:T(8,128)S(1)} %copy-done.5), kind=kOutput, calls=%fused_computation.26 | convolution fusion | flops 679477248 | bytes 1769472 | tf_op jit(solution)/shard_map/dot_general | solution.py:45
  87.7 0.0 all-gather.13.cloned.1.call-update
  87.7 0.8 fusion.1
  88.5 0.2 copy-done.2
  88.7 2.4 %fusion.6 = f32[384,384]{1,0:T(8,128)S(1)} fusion(f32[384,384]{1,0:T(8,128)S(1)} %fusion.1, f32[384,384]{1,0:T(8,128)S(1)} %copy-done.2, f32[384,384]{1,0:T(8,128)S(1)} %fusion.21, f32[384,384]{1,0:T(8,128)S(1)} %fusion.19, f32[384,384]{1,0:T(8,128)} %copy-done.3, pred[]{:T(512)S(6)} %gt.35, pred[]{:T(512)S(6)} %gt.34, pred[]{:T(512)S(6)} %gt.33, pred[]{:T(512)S(6)} %gt.32), kind=kOutput, calls=%fused_computation.10 | convolution fusion | flops 680361984 | bytes 3538948 | tf_op jit(solution)/shard_map/dot_general | solution.py:45
  91.1 38.4 %all-gather.13.cloned.1.call-done = f32[1536,384]{1,0:T(8,128)} async-done(((f32[384,384]{1,0:T(8,128)}), f32[1536,384]{1,0:T(8,128)}) %all-gather.13.cloned.1.call-update) | async-done | bytes 2359312 | tf_op jit(solution)/shard_map/all_gather | solution.py:19
  129.5 1.8 fusion.10
  131.4 2.3 %fusion.12 = f32[384,384]{1,0:T(8,128)S(1)} fusion(f32[384,384]{1,0:T(8,128)S(1)} %fusion.10, f32[1536,384]{1,0:T(8,128)} %all-gather.13.cloned.1.call-done), kind=kOutput, calls=%fused_computation.15 | convolution fusion | flops 679477248 | bytes 1769472 | tf_op jit(solution)/shard_map/dot_general | solution.py:45
  133.7 1.3 fusion.14
  135.0 0.0 copy-start.6
  135.0 1.3 convolution_select_fusion
  136.3 1.3 fusion.43
  137.6 0.4 fusion.38
  138.0 0.7 fusion.40
  138.7 0.1 reshape.3
  138.8 18.9 %all_to_all.5 = f32[32,12,384]{2,1,0:T(8,128)S(1)} all-to-all(f32[32,12,384]{2,1,0:T(8,128)S(1)} %reshape.3), channel_id=1, replica_groups=mesh['tm_0'=4,'tm_1'=4,'tm_2'=2,'group'=16] {'tm_0','tm_1','tm_2'}, dimensions={0} | all-to-all | bytes 1179648 | tf_op jit(solution)/shard_map/all_to_all | solution.py:36
  157.7 0.1 reduce_sum.18
  157.8 32.4 %all-gather.4 = f32[16,12,384]{2,1,0:T(8,128)S(1)} all-gather(f32[1,12,384]{2,1,0:T(8,128)S(1)} %bitcast.21), channel_id=5, replica_groups=mesh['tm_0'=4,'tm_1'=4,'tm_2'=2,'group'=16] {'group'}, dimensions={0}, use_global_device_ids=true | all-gather | bytes 313344 | tf_op jit(solution)/shard_map/all_gather | solution.py:41
  190.2 0.6 reduce_sum.19
  (12 shorter events, 0.0 us)
Async XLA Ops:
  6.5 1.1 copy-start
  6.5 27.0 %all-gather.9.cloned.1.call-start = ((), (), s32[]{:S(2)}) async-start(), calls=%async_computation.1 | async-start | bytes 1769472 | tf_op jit(solution)/shard_map/all_gather | solution.py:19
  9.2 70.6 %all-gather.11.cloned.1.call-start = ((), (), s32[]{:S(2)}) async-start(), calls=%async_computation.2 | async-start | bytes 2949120 | tf_op jit(solution)/shard_map/all_gather | solution.py:19
  38.6 91.0 %all-gather.13.cloned.1.call-start = ((), (), s32[]{:S(2)}) async-start(), calls=%async_computation.3 | async-start | bytes 2949120 | tf_op jit(solution)/shard_map/all_gather | solution.py:19
  79.8 4.4 %copy-start.5 = (f32[1536,384]{1,0:T(8,128)S(1)}, f32[1536,384]{1,0:T(8,128)}, u32[]{:S(2)}) copy-start(f32[1536,384]{1,0:T(8,128)} %all-gather.11.cloned.1.call-done) | copy-start | bytes 7077892
  81.7 3.8 %copy-start.3 = (f32[384,384]{1,0:T(8,128)}, f32[384,384]{1,0:T(8,128)S(1)}, u32[]{:S(2)}) copy-start(f32[384,384]{1,0:T(8,128)S(1)} %fusion.17) | copy-start | bytes 1769476
  84.3 3.4 %copy-start.1 = (f32[384,384]{1,0:T(8,128)S(1)}, f32[384,384]{1,0:T(8,128)}, u32[]{:S(2)}) copy-start(f32[384,384]{1,0:T(8,128)} %fusion.27) | copy-start | bytes 1769476
  87.7 1.1 copy-start.2
  129.5 4.2 %copy-start.4 = (f32[1536,384]{1,0:T(8,128)S(1)}, f32[1536,384]{1,0:T(8,128)}, u32[]{:S(2)}) copy-start(f32[1536,384]{1,0:T(8,128)} %all-gather.13.cloned.1.call-done) | copy-start | bytes 7077892
  135.0 2.6 %copy-start.6 = (f32[1,24,384]{2,1,0:T(8,128)S(1)}, f32[1,24,384]{2,1,0:T(8,128)}, u32[]{:S(2)}) copy-start(f32[1,24,384]{2,1,0:T(8,128)} %param.3) | copy-start | bytes 110596
Sparse Core Ops, SparseCore 0:
  9.4 24.0 all-gather.8
  38.7 41.1 all-gather.10
  87.8 41.6 all-gather.12
where the time goes:
time: 198 us; the launch traced here: 197 us
  waiting for transfers between devices  104 us (53%)
  blocking collectives  51.4 us (26%)
  matrix products  26.6 us (13%)
  between operations  13.3 us (7%)
    all_gather x3, waiting for transfers between devices, entering(): pieces = lax.all_gather(subtotal, axis)  104 us
    all_gather x1, blocking collectives, total_of_pieces(): return lax.all_gather(value, axis).sum(0)  32.4 us
    dot_general x16, matrix products, times_high(): jnp.dot(left, right, precision=lax.Precision.HIGHEST, preferred_element_t...  26.6 us
    all_to_all x1, blocking collectives, summed_on_arrival(): lax.all_to_all(parts, axis, split_axis=0, concat_axis=0, tiled=True)  18.9 us
  transfers between devices with their start and end apart: 3, of which 3 were waited for; matrix products, arithmetic and copies ran while one was open for 2% of the time, Pallas kernels for 0%

commit v1 on v0

v1 whole, which is shorter than its diff:
```python
import jax
import jax.numpy as jnp
from jax import lax
from jax.experimental import pallas as pl
from jax.experimental.pallas import tpu as pltpu
from jax.sharding import Mesh
from jax.sharding import PartitionSpec as P

AXES = ("x", "y", "c", "z")
MESH = pl.DeviceIdType.MESH
F32 = jnp.float32
BF16 = jnp.bfloat16
D = 384
HALF = D // 2
CHUNK = HALF // 2
NX = 4
NY = 4
NZ = 16
HB = D // NZ
ROWS = D // 32
PIECE = 16
WIDE = 8 * PIECE
NN = ((1,), (0,))
NT = ((1,), (1,))
TN = ((0,), (0,))


def parts(value):
    high = value.astype(BF16)
    return high, (value - high.astype(F32)).astype(BF16)


def bdot(left, right, dims):
    return lax.dot_general(left, right, (dims, ((), ())), preferred_element_type=F32)


def times(left, right, dims=NN):
    lh, ll = parts(left)
    rh, rl = parts(right)
    if dims is TN:
        return bdot(lh, rh, dims) + (bdot(ll, rh, dims) + bdot(lh, rl, dims))
    n = left.shape[0]
    both = bdot(jnp.concatenate([lh, ll], axis=0), rh, dims)
    return both[:n] + (both[n:] + bdot(lh, rl, dims))


def kernel(a_ref, h_ref, o_ref, ao, s_buf, r_buf, h_buf, l_buf, z_buf, u_buf, g_buf, e_buf,
           a_sem, ys_sem, yr_sem, yd_sem, ye_sem, xs_sem, xr_sem, xd_sem, xe_sem,
           hs_sem, hr_sem, gs_sem, gr_sem, es_sem, er_sem):
    x, y, c, z = (lax.axis_index(a) for a in AXES)
    xr, xl, xo = (lax.rem(x + k, NX) for k in (1, 3, 2))
    yr, yl, yo = (lax.rem(y + k, NY) for k in (1, 3, 2))
    zr, zl, zo = (lax.rem(z + k, NZ) for k in (1, NZ - 1, 2))
    sib = (x, y, 1 - c, z)
    right_y, left_y = (x, yr, c, z), (x, yl, c, z)
    right_x, left_x = (xr, y, c, z), (xl, y, c, z)
    right_z, left_z = (x, y, c, zr), (x, y, c, zl)

    barrier = pltpu.get_barrier_semaphore()
    for dev in (sib, right_y, left_y, right_x, left_x, right_z, left_z):
        pl.semaphore_signal(barrier, 1, device_id=dev, device_id_type=MESH)
    pl.semaphore_wait(barrier, 7)

    def remote(src, dst, send, recv, dev):
        return pltpu.make_async_remote_copy(
            src_ref=src, dst_ref=dst, send_sem=send, recv_sem=recv, device_id=dev, device_id_type=MESH)

    a_copy = remote(a_ref.at[0], ao, a_sem.at[0], a_sem.at[1], sib)
    a_copy.start()
    h_buf[pl.ds(z * HB, HB)] = h_ref[0]

    def h_block(k):
        return h_buf.at[pl.ds(lax.rem(z + k + NZ, NZ) * HB, HB)]

    def h_right(j):
        return remote(h_block(-j), h_block(-j), hs_sem.at[0, j], hr_sem.at[0, j], right_z)

    def h_left(j):
        return remote(h_block(j), h_block(j), hs_sem.at[1, j], hr_sem.at[1, j], left_z)

    def h_wait_right(j):
        remote(h_block(-j), h_block(-j), hs_sem.at[0, j - 1], hr_sem.at[0, j - 1], right_z).wait_recv()

    def h_wait_left(j):
        remote(h_block(j), h_block(j), hs_sem.at[1, j - 1], hr_sem.at[1, j - 1], left_z).wait_recv()

    def h_step(j):
        h_wait_right(j)
        if j < NZ // 2:
            h_right(j).start()
            h_wait_left(j)
            if j < NZ // 2 - 1:
                h_left(j).start()

    h_right(0).start()
    h_left(0).start()
    a_copy.wait_recv()

    half = pl.ds(c * HALF, HALF)

    @pl.when(c == 0)
    def _():
        s_buf[y, half] = times(ao[half], a_ref[0])

    @pl.when(c == 1)
    def _():
        s_buf[y, half] = times(a_ref[0, half], ao[...])

    def rows(k, core=None):
        return pl.ds((c if core is None else core) * HALF + k * CHUNK, CHUNK)

    def s_chunk(place, k):
        return s_buf.at[place, rows(k)]

    def y_copy(place, k, dev, n):
        return remote(s_chunk(place, k), s_chunk(place, k), ys_sem.at[n], yr_sem.at[n], dev)

    def y_share(place, k, n):
        return remote(s_chunk(place, k), s_chunk(place, k), yd_sem.at[n], ye_sem.at[n], sib)

    def y_shared(place, k, n):
        there = s_buf.at[place, rows(k, 1 - c)]
        return remote(there, there, yd_sem.at[n], ye_sem.at[n], sib)

    y_out = [
        y_copy(y, 0, right_y, 0), y_copy(y, 1, left_y, 3),
        y_copy(y, 1, right_y, 1), y_copy(y, 0, left_y, 2),
    ]
    for copy in y_out:
        copy.start()
    y_sh = []

    def share_s(place, k, n):
        copy = y_share(place, k, n)
        copy.start()
        y_sh.append((copy, y_shared(place, k, n)))

    share_s(y, 0, 6)
    share_s(y, 1, 7)
    h_step(1)
    y_copy(yl, 0, left_y, 0).wait_recv()
    copy = y_copy(yl, 0, right_y, 4)
    copy.start()
    y_out.append(copy)
    y_copy(yr, 1, right_y, 3).wait_recv()
    copy = y_copy(yr, 1, left_y, 5)
    copy.start()
    y_out.append(copy)
    share_s(yl, 0, 0)
    share_s(yr, 1, 3)
    h_step(2)
    y_copy(yl, 1, left_y, 1).wait_recv()
    share_s(yl, 1, 1)
    y_copy(yr, 0, left_y, 2).wait_recv()
    share_s(yr, 0, 2)
    h_step(3)
    y_copy(yo, 0, left_y, 4).wait_recv()
    share_s(yo, 0, 4)
    y_copy(yo, 1, left_y, 5).wait_recv()
    share_s(yo, 1, 5)
    for _, arrival in y_sh:
        arrival.wait_recv()

    @pl.when(x < NX - 1)
    def _():
        value = s_buf[3, half]
        for k in (2, 1, 0):
            value = times(value, s_buf[k])
        r_buf[x, half] = value

    def r_chunk(place, k):
        return r_buf.at[place, rows(k)]

    def x_copy(place, k, dev, n):
        return remote(r_chunk(place, k), r_chunk(place, k), xs_sem.at[n], xr_sem.at[n], dev)

    def x_share(place, k, n):
        return remote(r_chunk(place, k), r_chunk(place, k), xd_sem.at[n], xe_sem.at[n], sib)

    def x_shared(place, k, n):
        there = r_buf.at[place, rows(k, 1 - c)]
        return remote(there, there, xd_sem.at[n], xe_sem.at[n], sib)

    to_right = x < 3
    first = x == 0
    last = x == 3
    x_out = []

    def when_start(cond, copy):
        @pl.when(cond)
        def _():
            copy.start()
        x_out.append((cond, copy))

    def when_recv(cond, copy):
        @pl.when(cond)
        def _():
            copy.wait_recv()

    when_start(to_right, x_copy(x, 0, right_x, 0))
    when_start(x < 2, x_copy(x, 1, left_x, 3))
    when_start(to_right, x_copy(x, 1, right_x, 1))
    when_start(first, x_copy(x, 0, left_x, 2))
    h_step(4)

    @pl.when(y == 1)
    def _():
        l_buf[...] = s_buf[0]

    @pl.when(y >= 2)
    def _():
        l_buf[...] = times(s_buf[1], s_buf[0])

    x_sh = []

    def share_r(cond, place, k, n):
        copy = x_share(place, k, n)
        when_start(cond, copy)
        x_sh.append((cond, x_shared(place, k, n)))

    from_left = x > 0
    opposite = x > 1
    when_recv(from_left, x_copy(xl, 0, left_x, 0))
    when_start((x == 1) | (x == 2), x_copy(xl, 0, right_x, 4))
    when_recv(first | last, x_copy(xr, 1, right_x, 3))
    when_start(first | last, x_copy(xr, 1, left_x, 5))
    share_r(from_left, xl, 0, 0)
    share_r(last, xr, 1, 3)
    h_step(5)

    @pl.when(y == 3)
    def _():
        l_buf[...] = times(s_buf[2], l_buf[...])

    @pl.when((c == 1) & (y == 0))
    def _():
        l_buf[...] = ao[...]

    @pl.when((c == 1) & (y > 0))
    def _():
        l_buf[...] = times(ao[...], l_buf[...])

    h_step(6)
    when_recv(from_left, x_copy(xl, 1, left_x, 1))
    share_r(from_left, xl, 1, 1)
    when_recv(last, x_copy(xr, 0, left_x, 2))
    share_r(last, xr, 0, 2)
    h_step(7)
    when_recv(opposite, x_copy(xo, 0, left_x, 4))
    share_r(opposite, xo, 0, 4)
    when_recv(opposite, x_copy(xo, 1, left_x, 5))
    share_r(opposite, xo, 1, 5)
    h_step(8)

    inner = (y > 0) | (c > 0)

    @pl.when(jnp.logical_not(inner))
    def _():
        z_buf[...] = h_buf[...]

    @pl.when(inner)
    def _():
        z_buf[...] = times(l_buf[...], times(h_buf[...], l_buf[...]), TN)

    for cond, arrival in x_sh:
        when_recv(cond, arrival)

    part = lax.rem(z, 4)
    place = lax.broadcasted_iota(jnp.int32, (WIDE, D), 0)
    column = lax.broadcasted_iota(jnp.int32, (WIDE, D), 1)
    within = place & (PIECE - 1)
    wanted = part * (8 * ROWS) + (place >> 4) * ROWS + within
    u_buf[...] = jnp.where((within < ROWS) & (column == wanted), 1.0, 0.0).astype(F32)
    for k in range(NX - 1):
        @pl.when(x > k)
        def _(k=k):
            u_buf[...] = times(u_buf[...], r_buf[k], NT)
    u_buf[...] = times(u_buf[...], z_buf[...])
    for k in reversed(range(NX - 1)):
        @pl.when(x > k)
        def _(k=k):
            u_buf[...] = times(u_buf[...], r_buf[k])

    me = (x * NY + y) * 2 + c
    owner = x == part
    g_out = []
    for p in range(8):
        mine = owner & (y * 2 + c == p)
        copy = remote(u_buf.at[pl.ds(p * PIECE, PIECE)], g_buf.at[me], gs_sem.at[p], gr_sem.at[me],
                      (part, p // 2, p % 2, z))

        @pl.when(mine)
        def _(p=p):
            g_buf[me] = u_buf[pl.ds(p * PIECE, PIECE)]

        @pl.when(jnp.logical_not(mine))
        def _(copy=copy):
            copy.start()
        g_out.append((jnp.logical_not(mine), copy))

    e_out = [remote(e_buf.at[0], e_buf.at[1], es_sem.at[k], er_sem.at[0], (x, y, c, dev))
             for k, dev in enumerate((zr, zl, zo))]

    @pl.when(owner)
    def _():
        for s in range(32):
            @pl.when(s != me)
            def _(s=s):
                remote(g_buf.at[s], g_buf.at[s], gs_sem.at[0], gr_sem.at[s], sib).wait_recv()
        total = g_buf[0]
        for s in range(1, 32):
            total = total + g_buf[s]
        e_buf[0] = total
        for copy in e_out:
            copy.start()
        o_ref[...] = total[:ROWS]
        for copy in e_out:
            copy.wait_send()

    @pl.when(jnp.logical_not(owner))
    def _():
        e_out[0].wait_recv()
        o_ref[...] = e_buf[1, :ROWS]

    a_copy.wait_send()
    for j in range(NZ // 2):
        h_right(j).wait_send()
    for j in range(NZ // 2 - 1):
        h_left(j).wait_send()
    for copy in y_out:
        copy.wait_send()
    for copy, _ in y_sh:
        copy.wait_send()
    for cond, copy in x_out + g_out:
        @pl.when(cond)
        def _(copy=copy):
            copy.wait_send()


def body(propagators, perturbation):
    full = pltpu.VMEM((D, D), F32)
    dma = pltpu.SemaphoreType.DMA
    return pl.pallas_call(
        kernel,
        out_shape=jax.ShapeDtypeStruct((ROWS, D), F32),
        in_specs=[pl.BlockSpec(memory_space=pltpu.VMEM)] * 2,
        out_specs=pl.BlockSpec(memory_space=pltpu.VMEM),
        scratch_shapes=[
            full,
            pltpu.VMEM((NY, D, D), F32),
            pltpu.VMEM((NX, D, D), F32),
            full,
            full,
            full,
            pltpu.VMEM((WIDE, D), F32),
            pltpu.VMEM((32, PIECE, D), F32),
            pltpu.VMEM((2, PIECE, D), F32),
            dma((2,)),
            dma((6,)), dma((6,)), dma((8,)), dma((8,)),
            dma((6,)), dma((6,)), dma((6,)), dma((6,)),
            dma((2, 8)), dma((2, 8)),
            dma((8,)), dma((32,)),
            dma((3,)), dma((1,)),
        ],
        compiler_params=pltpu.CompilerParams(
            collective_id=0, has_side_effects=True, vmem_limit_bytes=48 * 2**20),
        name="floquet",
    )(propagators, perturbation)


def solution(mesh):
    split = Mesh(mesh.devices.reshape(NX, NY, 2, NZ), AXES)
    tm = ("x", "y", "c")
    return jax.shard_map(
        body,
        mesh=split,
        in_specs=(P(tm, None, None), P(tm, "z", None)),
        out_specs=P(tm, None),
        check_vma=False,
    )
```

time: 198 us -> 62.3 us (0.31)
  the two profiles are of different devices: /device:TPU:8 before, /device:TPU:28 now
where the time goes in v1:
time: 62.3 us; the launch traced here: 62.1 us
  Pallas kernels  59.6 us (96%)
  local copies, waits for them, and re-layouts  2.44 us (4%)
    pallas_call x1, Pallas kernels, body(): pl.pallas_call(kernel, out_shape=jax.ShapeDtypeStruct((ROWS, D), F32), in...  59.6 us
    unnamed x5, local copies, waits for them, and re-layouts  2.44 us

profile of v1, /device:TPU:28, one launch (start us, length us, event | category | flops | bytes accessed | tf_op | source)
XLA Modules:
  0.0 62.1 jit_solution(6013288033888795155)
XLA Ops:
  0.0 0.0 copy-start
  0.0 1.1 %copy-done = f32[1,384,384]{2,1,0:T(8,128)S(1)} copy-done((f32[1,384,384]{2,1,0:T(8,128)S(1)}, f32[1,384,384]{2,1,0:T(8,128)}, u32[]{:S(2)}) %copy-start) | copy-done | bytes 589848
  1.1 0.0 copy-start.1
  1.1 0.8 %copy-done.1 = f32[1,24,384]{2,1,0:T(8,128)S(1)} copy-done((f32[1,24,384]{2,1,0:T(8,128)S(1)}, f32[1,24,384]{2,1,0:T(8,128)}, u32[]{:S(2)}) %copy-start.1) | copy-done | bytes 36888
  1.8 59.6 %floquet.1 = f32[12,384]{1,0:T(8,128)S(1)} custom-call(f32[1,384,384]{2,1,0:T(8,128)S(1)} %copy-done, f32[1,24,384]{2,1,0:T(8,128)S(1)} %copy-done.1), custom_call_target="tpu_custom_call" | custom-call | tf_op jit(solution)/shard_map/floquet/pallas_call | solution.py:343
  61.5 0.6 copy.4
Async XLA Ops:
  0.0 1.1 %copy-start = (f32[1,384,384]{2,1,0:T(8,128)S(1)}, f32[1,384,384]{2,1,0:T(8,128)}, u32[]{:S(2)}) copy-start(f32[1,384,384]{2,1,0:T(8,128)} %a_ref.1) | copy-start | bytes 1769476
  1.1 0.8 %copy-start.1 = (f32[1,24,384]{2,1,0:T(8,128)S(1)}, f32[1,24,384]{2,1,0:T(8,128)}, u32[]{:S(2)}) copy-start(f32[1,24,384]{2,1,0:T(8,128)} %h_ref.1) | copy-start | bytes 110596

commit v2 on v1

--- a/solution.py
+++ b/solution.py
@@ -19,7 +19,7 @@
 HB = D // NZ
 ROWS = D // 32
 PIECE = 16
-WIDE = 8 * PIECE
+WIDE = 4 * PIECE
 NN = ((1,), (0,))
 NT = ((1,), (1,))
 TN = ((0,), (0,))
@@ -44,10 +44,14 @@
     return both[:n] + (both[n:] + bdot(lh, rl, dims))
 
 
-def kernel(a_ref, h_ref, o_ref, ao, s_buf, r_buf, h_buf, l_buf, z_buf, u_buf, g_buf, e_buf,
-           a_sem, ys_sem, yr_sem, yd_sem, ye_sem, xs_sem, xr_sem, xd_sem, xe_sem,
-           hs_sem, hr_sem, gs_sem, gr_sem, es_sem, er_sem):
+def kernel(a_hbm, h_hbm, o_ref, av, ao, s_buf, r_buf, h_buf, l_buf, z_buf, zo_buf, u_buf, t_buf, v_buf, g_buf,
+           in_sem, a_sem, ys_sem, yr_sem, yd_sem, ye_sem, xs_sem, xr_sem, xd_sem, xe_sem,
+           hs_sem, hr_sem, zz_sem, ts_sem, tr_sem, gs_sem, gr_sem):
     x, y, c, z = (lax.axis_index(a) for a in AXES)
+    a_load = pltpu.make_async_copy(a_hbm.at[0], av, in_sem.at[0])
+    h_load = pltpu.make_async_copy(h_hbm.at[0], h_buf.at[pl.ds(z * HB, HB)], in_sem.at[1])
+    a_load.start()
+    h_load.start()
     xr, xl, xo = (lax.rem(x + k, NX) for k in (1, 3, 2))
     yr, yl, yo = (lax.rem(y + k, NY) for k in (1, 3, 2))
     zr, zl, zo = (lax.rem(z + k, NZ) for k in (1, NZ - 1, 2))
@@ -65,9 +69,16 @@
         return pltpu.make_async_remote_copy(
             src_ref=src, dst_ref=dst, send_sem=send, recv_sem=recv, device_id=dev, device_id_type=MESH)
 
-    a_copy = remote(a_ref.at[0], ao, a_sem.at[0], a_sem.at[1], sib)
-    a_copy.start()
-    h_buf[pl.ds(z * HB, HB)] = h_ref[0]
+    low, high = pl.ds(0, HALF), pl.ds(HALF, HALF)
+    a_low = remote(av.at[low], ao.at[low], a_sem.at[0], a_sem.at[1], sib)
+    a_high = remote(av.at[high], ao.at[high], a_sem.at[2], a_sem.at[3], sib)
+    a_load.wait()
+    a_low.start()
+
+    @pl.when(c == 0)
+    def _():
+        a_high.start()
+    h_load.wait()
 
     def h_block(k):
         return h_buf.at[pl.ds(lax.rem(z + k + NZ, NZ) * HB, HB)]
@@ -94,17 +105,18 @@
 
     h_right(0).start()
     h_left(0).start()
-    a_copy.wait_recv()
+    a_low.wait_recv()
 
     half = pl.ds(c * HALF, HALF)
 
     @pl.when(c == 0)
     def _():
-        s_buf[y, half] = times(ao[half], a_ref[0])
+        s_buf[y, low] = times(ao[low], av[...])
 
     @pl.when(c == 1)
     def _():
-        s_buf[y, half] = times(a_ref[0, half], ao[...])
+        a_high.wait_recv()
+        s_buf[y, high] = times(av[high], ao[...])
 
     def rows(k, core=None):
         return pl.ds((c if core is None else core) * HALF + k * CHUNK, CHUNK)
@@ -138,6 +150,7 @@
     share_s(y, 0, 6)
     share_s(y, 1, 7)
     h_step(1)
+    h_step(2)
     y_copy(yl, 0, left_y, 0).wait_recv()
     copy = y_copy(yl, 0, right_y, 4)
     copy.start()
@@ -148,12 +161,12 @@
     y_out.append(copy)
     share_s(yl, 0, 0)
     share_s(yr, 1, 3)
-    h_step(2)
+    h_step(3)
     y_copy(yl, 1, left_y, 1).wait_recv()
     share_s(yl, 1, 1)
     y_copy(yr, 0, left_y, 2).wait_recv()
     share_s(yr, 0, 2)
-    h_step(3)
+    h_step(4)
     y_copy(yo, 0, left_y, 4).wait_recv()
     share_s(yo, 0, 4)
     y_copy(yo, 1, left_y, 5).wait_recv()
@@ -201,7 +214,7 @@
     when_start(x < 2, x_copy(x, 1, left_x, 3))
     when_start(to_right, x_copy(x, 1, right_x, 1))
     when_start(first, x_copy(x, 0, left_x, 2))
-    h_step(4)
+    h_step(5)
 
     @pl.when(y == 1)
     def _():
@@ -210,6 +223,8 @@
     @pl.when(y >= 2)
     def _():
         l_buf[...] = times(s_buf[1], s_buf[0])
+
+    h_step(6)
 
     x_sh = []
 
@@ -226,7 +241,7 @@
     when_start(first | last, x_copy(xr, 1, left_x, 5))
     share_r(from_left, xl, 0, 0)
     share_r(last, xr, 1, 3)
-    h_step(5)
+    h_step(7)
 
     @pl.when(y == 3)
     def _():
@@ -240,28 +255,28 @@
     def _():
         l_buf[...] = times(ao[...], l_buf[...])
 
-    h_step(6)
+    h_step(8)
     when_recv(from_left, x_copy(xl, 1, left_x, 1))
     share_r(from_left, xl, 1, 1)
     when_recv(last, x_copy(xr, 0, left_x, 2))
     share_r(last, xr, 0, 2)
-    h_step(7)
+
+    inner = (y > 0) | (c > 0)
+
+    @pl.when(jnp.logical_not(inner))
+    def _():
+        z_buf[...] = h_buf[...]
+
+    @pl.when(inner)
+    def _():
+        z_buf[...] = times(l_buf[...], times(h_buf[...], l_buf[...]), TN)
+
+    z_copy = remote(z_buf, zo_buf, zz_sem.at[0], zz_sem.at[1], sib)
+    z_copy.start()
     when_recv(opposite, x_copy(xo, 0, left_x, 4))
     share_r(opposite, xo, 0, 4)
     when_recv(opposite, x_copy(xo, 1, left_x, 5))
     share_r(opposite, xo, 1, 5)
-    h_step(8)
-
-    inner = (y > 0) | (c > 0)
-
-    @pl.when(jnp.logical_not(inner))
-    def _():
-        z_buf[...] = h_buf[...]
-
-    @pl.when(inner)
-    def _():
-        z_buf[...] = times(l_buf[...], times(h_buf[...], l_buf[...]), TN)
-
     for cond, arrival in x_sh:
         when_recv(cond, arrival)
 
@@ -269,60 +284,70 @@
     place = lax.broadcasted_iota(jnp.int32, (WIDE, D), 0)
     column = lax.broadcasted_iota(jnp.int32, (WIDE, D), 1)
     within = place & (PIECE - 1)
-    wanted = part * (8 * ROWS) + (place >> 4) * ROWS + within
+    wanted = part * (8 * ROWS) + (c * 4 + (place >> 4)) * ROWS + within
     u_buf[...] = jnp.where((within < ROWS) & (column == wanted), 1.0, 0.0).astype(F32)
     for k in range(NX - 1):
         @pl.when(x > k)
         def _(k=k):
             u_buf[...] = times(u_buf[...], r_buf[k], NT)
-    u_buf[...] = times(u_buf[...], z_buf[...])
+    z_copy.wait_recv()
+    u_buf[...] = times(u_buf[...], z_buf[...] + zo_buf[...])
+
+    t_out = []
+    for q in range(4):
+        yt, ct = c * 2 + q // 2, q % 2
+        mine = (y == yt) & (c == ct)
+        copy = remote(u_buf.at[pl.ds(q * PIECE, PIECE)], t_buf.at[y], ts_sem.at[q], tr_sem.at[y],
+                      (x, yt, ct, z))
+
+        @pl.when(mine)
+        def _(q=q):
+            t_buf[y] = u_buf[pl.ds(q * PIECE, PIECE)]
+
+        @pl.when(jnp.logical_not(mine))
+        def _(copy=copy):
+            copy.start()
+        t_out.append((jnp.logical_not(mine), copy))
+    holder = c == lax.div(y, 2)
+    for k in range(NY):
+        @pl.when(jnp.logical_not(holder & (y == k)))
+        def _(k=k):
+            remote(t_buf.at[k], t_buf.at[k], ts_sem.at[0], tr_sem.at[k], sib).wait_recv()
+    v_buf[...] = (t_buf[0] + t_buf[1]) + (t_buf[2] + t_buf[3])
     for k in reversed(range(NX - 1)):
         @pl.when(x > k)
         def _(k=k):
-            u_buf[...] = times(u_buf[...], r_buf[k])
-
-    me = (x * NY + y) * 2 + c
-    owner = x == part
-    g_out = []
-    for p in range(8):
-        mine = owner & (y * 2 + c == p)
-        copy = remote(u_buf.at[pl.ds(p * PIECE, PIECE)], g_buf.at[me], gs_sem.at[p], gr_sem.at[me],
-                      (part, p // 2, p % 2, z))
-
-        @pl.when(mine)
-        def _(p=p):
-            g_buf[me] = u_buf[pl.ds(p * PIECE, PIECE)]
-
-        @pl.when(jnp.logical_not(mine))
-        def _(copy=copy):
+            v_buf[...] = times(v_buf[...], r_buf[k])
+
+    for k, there in enumerate((z, zr, zl, zo)):
+        copy = remote(v_buf, g_buf.at[x], gs_sem.at[k], gr_sem.at[x], (part, y, c, there))
+        if k == 0:
+            cond = x != part
+
+            @pl.when(x == part)
+            def _():
+                g_buf[x] = v_buf[...]
+
+            @pl.when(cond)
+            def _(copy=copy):
+                copy.start()
+            t_out.append((cond, copy))
+        else:
             copy.start()
-        g_out.append((jnp.logical_not(mine), copy))
-
-    e_out = [remote(e_buf.at[0], e_buf.at[1], es_sem.at[k], er_sem.at[0], (x, y, c, dev))
-             for k, dev in enumerate((zr, zl, zo))]
-
-    @pl.when(owner)
-    def _():
-        for s in range(32):
-            @pl.when(s != me)
-            def _(s=s):
-                remote(g_buf.at[s], g_buf.at[s], gs_sem.at[0], gr_sem.at[s], sib).wait_recv()
-        total = g_buf[0]
-        for s in range(1, 32):
-            total = total + g_buf[s]
-        e_buf[0] = total
-        for copy in e_out:
-            copy.start()
-        o_ref[...] = total[:ROWS]
-        for copy in e_out:
-            copy.wait_send()
-
-    @pl.when(jnp.logical_not(owner))
-    def _():
-        e_out[0].wait_recv()
-        o_ref[...] = e_buf[1, :ROWS]
-
-    a_copy.wait_send()
+            t_out.append((c < 2, copy))
+    for k in range(NX):
+        @pl.when(jnp.logical_not((x == part) & (x == k)))
+        def _(k=k):
+            remote(g_buf.at[k], g_buf.at[k], gs_sem.at[0], gr_sem.at[k], sib).wait_recv()
+    total = (g_buf[0] + g_buf[1]) + (g_buf[2] + g_buf[3])
+    o_ref[...] = total[:ROWS]
+
+    a_low.wait_send()
+
+    @pl.when(c == 0)
+    def _():
+        a_high.wait_send()
+    z_copy.wait_send()
     for j in range(NZ // 2):
         h_right(j).wait_send()
     for j in range(NZ // 2 - 1):
@@ -331,7 +356,7 @@
         copy.wait_send()
     for copy, _ in y_sh:
         copy.wait_send()
-    for cond, copy in x_out + g_out:
+    for cond, copy in x_out + t_out:
         @pl.when(cond)
         def _(copy=copy):
             copy.wait_send()
@@ -343,27 +368,26 @@
     return pl.pallas_call(
         kernel,
         out_shape=jax.ShapeDtypeStruct((ROWS, D), F32),
-        in_specs=[pl.BlockSpec(memory_space=pltpu.VMEM)] * 2,
+        in_specs=[pl.BlockSpec(memory_space=pltpu.HBM)] * 2,
         out_specs=pl.BlockSpec(memory_space=pltpu.VMEM),
         scratch_shapes=[
-            full,
+            full, full,
             pltpu.VMEM((NY, D, D), F32),
             pltpu.VMEM((NX, D, D), F32),
-            full,
-            full,
-            full,
+            full, full, full, full,
             pltpu.VMEM((WIDE, D), F32),
-            pltpu.VMEM((32, PIECE, D), F32),
-            pltpu.VMEM((2, PIECE, D), F32),
-            dma((2,)),
+            pltpu.VMEM((NY, PIECE, D), F32),
+            pltpu.VMEM((PIECE, D), F32),
+            pltpu.VMEM((NX, PIECE, D), F32),
+            dma((2,)), dma((4,)),
             dma((6,)), dma((6,)), dma((8,)), dma((8,)),
             dma((6,)), dma((6,)), dma((6,)), dma((6,)),
-            dma((2, 8)), dma((2, 8)),
-            dma((8,)), dma((32,)),
-            dma((3,)), dma((1,)),
+            dma((2, 8)), dma((2, 8)), dma((2,)),
+            dma((4,)), dma((4,)),
+            dma((4,)), dma((4,)),
         ],
         compiler_params=pltpu.CompilerParams(
-            collective_id=0, has_side_effects=True, vmem_limit_bytes=48 * 2**20),
+            collective_id=0, has_side_effects=True, vmem_limit_bytes=60 * 2**20),
         name="floquet",
     )(propagators, perturbation)
 

time: 62.3 us -> 54.8 us (0.88)
  the two profiles are of different devices: /device:TPU:28 before, /device:TPU:1 now
where the time goes in v2:
time: 54.8 us; the launch traced here: 53.8 us
  Pallas kernels  52.4 us (96%)
  local copies, waits for them, and re-layouts  1.35 us (2%)
    pallas_call x1, Pallas kernels, body(): pl.pallas_call(kernel, out_shape=jax.ShapeDtypeStruct((ROWS, D), F32), in...  52.4 us
    unnamed x1, local copies, waits for them, and re-layouts  1.35 us

profile of v2, /device:TPU:1, one launch (start us, length us, event | category | flops | bytes accessed | tf_op | source)
XLA Modules:
  0.0 53.8 jit_solution(11111429597382180370)
XLA Ops:
  0.0 52.4 %floquet.1 = f32[12,384]{1,0:T(8,128)} custom-call(f32[1,384,384]{2,1,0:T(8,128)} %a_hbm.1, f32[1,24,384]{2,1,0:T(8,128)} %h_hbm.1), custom_call_target="tpu_custom_call" | custom-call | tf_op jit(solution)/shard_map/floquet/pallas_call | solution.py:368
  52.4 1.3 %copy.4 = f32[12,384]{1,0:T(8,128)} copy(f32[12,384]{1,0:T(8,128)} %floquet.1) | data formatting | bytes 36864

commit v3 on v0

v3 whole, which is shorter than its diff:
```python
import jax
import jax.numpy as jnp
from jax import lax
from jax.experimental import pallas as pl
from jax.experimental.pallas import tpu as pltpu
from jax.sharding import Mesh
from jax.sharding import PartitionSpec as P

AXES = ("x", "y", "c", "z")
MESH = pl.DeviceIdType.MESH
F32 = jnp.float32
BF16 = jnp.bfloat16
D = 384
HALF = D // 2
CHUNK = HALF // 2
PART = CHUNK // 2
NX = 4
NY = 4
NZ = 16
NW = 4
HB = D // NZ
ROWS = D // 32
PIECE = 16
WIDE = 4 * PIECE
NN = ((1,), (0,))
NT = ((1,), (1,))
TN = ((0,), (0,))


def parts(value):
    high = value.astype(BF16)
    return high, (value - high.astype(F32)).astype(BF16)


def bdot(left, right, dims):
    return lax.dot_general(left, right, (dims, ((), ())), preferred_element_type=F32)


def times(left, right, dims=NN):
    lh, ll = parts(left)
    rh, rl = parts(right)
    if dims is TN:
        return bdot(lh, rh, dims) + (bdot(ll, rh, dims) + bdot(lh, rl, dims))
    n = left.shape[0]
    both = bdot(jnp.concatenate([lh, ll], axis=0), rh, dims)
    return both[:n] + (both[n:] + bdot(lh, rl, dims))


def kernel(a_hbm, h_hbm, o_ref, av, ao, s_buf, r_buf, h_buf, l_buf, z_buf, zo_buf, u_buf, t_buf, v_buf, g_buf, n_buf,
           e_buf, in_sem, a_sem, ys_sem, yr_sem, yd_sem, ye_sem, xs_sem, xr_sem, xd_sem, xe_sem,
           hs_sem, hr_sem, zz_sem, ts_sem, tr_sem, gs_sem, gr_sem, es_sem, er_sem):
    x, y, c, z = (lax.axis_index(a) for a in AXES)
    worker = z < NW
    owner = z == x
    here = pl.ds(z * HB, HB)
    a_load = pltpu.make_async_copy(a_hbm.at[0], av, in_sem.at[0])
    h_load = pltpu.make_async_copy(h_hbm.at[0], h_buf.at[here], in_sem.at[1])
    pl.when(worker)(a_load.start)
    h_load.start()
    xr, xl, xo = (lax.rem(x + k, NX) for k in (1, 3, 2))
    yr, yl, yo = (lax.rem(y + k, NY) for k in (1, 3, 2))
    others = [(x, y, c, lax.rem(z + k, NZ)) for k in range(1, NZ)]
    sib = (x, y, 1 - c, z)
    right_y, left_y = (x, yr, c, z), (x, yl, c, z)
    right_x, left_x = (xr, y, c, z), (xl, y, c, z)

    barrier = pltpu.get_barrier_semaphore()

    @pl.when(worker)
    def _():
        for dev in [sib, right_y, left_y, right_x, left_x] + others:
            pl.semaphore_signal(barrier, 1, device_id=dev, device_id_type=MESH)
        pl.semaphore_wait(barrier, 5 + NW - 1)

    @pl.when(jnp.logical_not(worker))
    def _():
        pl.semaphore_wait(barrier, NW)

    def remote(src, dst, send, recv, dev):
        return pltpu.make_async_remote_copy(
            src_ref=src, dst_ref=dst, send_sem=send, recv_sem=recv, device_id=dev, device_id_type=MESH)

    h_out = [remote(h_buf.at[here], h_buf.at[here], hs_sem.at[k], hr_sem.at[0], (x, y, c, k)) for k in range(NW)]

    def send_rows():
        h_load.wait()
        for k, copy in enumerate(h_out):
            pl.when(z != k)(copy.start)

    e_out = [remote(e_buf.at[0], e_buf.at[1], es_sem.at[k], er_sem.at[0], dev)
             for k, dev in enumerate(others)]

    def work():
        low, high = pl.ds(0, HALF), pl.ds(HALF, HALF)
        low0, low1 = pl.ds(0, CHUNK), pl.ds(CHUNK, CHUNK)
        half = pl.ds(c * HALF, HALF)

        def a_copies(*where):
            return [remote(av.at[w], ao.at[w], a_sem.at[k], a_sem.at[2 + k], sib) for k, w in enumerate(where)]

        a_down = a_copies(low0, low1)
        a_up = a_copies(low, high)
        a_load.wait()

        @pl.when(c == 0)
        def _():
            for copy in a_up:
                copy.start()

        @pl.when(c == 1)
        def _():
            for copy in a_down:
                copy.start()
        send_rows()

        def rows(k, core=None):
            return pl.ds((c if core is None else core) * HALF + k * CHUNK, CHUNK)

        def subrows(k, core=None):
            return pl.ds((c if core is None else core) * HALF + k * PART, PART)

        def gather(buf, out_sem, in_sem, share_out, share_in, right, left):
            def copy(place, k, dev, n):
                there = buf.at[place, rows(k) if n < 4 else subrows(k)]
                return remote(there, there, out_sem.at[n], in_sem.at[n], dev)

            def share(place, k, n):
                there = buf.at[place, subrows(k) if 4 <= n < 8 else rows(k)]
                return remote(there, there, share_out.at[n], share_in.at[n], sib)

            def shared(place, k, n):
                there = buf.at[place, subrows(k, 1 - c) if 4 <= n < 8 else rows(k, 1 - c)]
                return remote(there, there, share_out.at[n], share_in.at[n], sib)

            return copy, share, shared

        y_copy, y_share, y_shared = gather(s_buf, ys_sem, yr_sem, yd_sem, ye_sem, right_y, left_y)
        y_out = [
            y_copy(y, 0, right_y, 0), y_copy(y, 1, left_y, 3),
            y_copy(y, 1, right_y, 1), y_copy(y, 0, left_y, 2),
        ]
        y_sh = {}

        def share_s(place, k, n):
            copy = y_share(place, k, n)
            copy.start()
            y_sh[n] = (copy, y_shared(place, k, n))

        @pl.when(c == 0)
        def _():
            a_down[0].wait_recv()
            s_buf[y, low0] = times(ao[low0], av[...])
            y_out[0].start()
            a_down[1].wait_recv()
            s_buf[y, low1] = times(ao[low1], av[...])

        @pl.when(c == 1)
        def _():
            for copy in a_up:
                copy.wait_recv()
            s_buf[y, high] = times(av[high], ao[...])
            y_out[0].start()

        for copy in y_out[1:]:
            copy.start()
        share_s(y, 0, 8)
        share_s(y, 1, 9)

        def relay(k, source, dev, n):
            for m in range(2):
                copy = y_copy(source, 2 * k + m, dev, n + m)
                copy.start()
                y_out.append(copy)

        y_copy(yl, 0, left_y, 0).wait_recv()
        relay(0, yl, right_y, 4)
        y_copy(yr, 1, right_y, 3).wait_recv()
        relay(1, yr, left_y, 6)
        share_s(yl, 0, 0)
        share_s(yr, 1, 3)
        y_copy(yl, 1, left_y, 1).wait_recv()
        share_s(yl, 1, 1)
        y_copy(yr, 0, left_y, 2).wait_recv()
        share_s(yr, 0, 2)
        for k, n in ((0, 4), (2, 6), (1, 5), (3, 7)):
            y_copy(yo, k, left_y, n).wait_recv()
            share_s(yo, k, n)

        for n in (8, 9, 0, 3, 1, 2):
            y_sh[n][1].wait_recv()

        ahead = x < NX - 1

        @pl.when(ahead & (y == 0))
        def _():
            z_buf[...] = times(s_buf[1], s_buf[0])

        @pl.when(ahead & (y == 1))
        def _():
            z_buf[...] = times(s_buf[2], times(s_buf[1], s_buf[0]))

        @pl.when(ahead & (y >= 2))
        def _():
            n_buf[...] = times(s_buf[3, half], s_buf[2])

        @pl.when(ahead & (y == 2))
        def _():
            n_buf[...] = times(n_buf[...], s_buf[1])

        def opposite_shared():
            for n in (4, 6, 5, 7):
                y_sh[n][1].wait_recv()

        pl.when(y != 1)(opposite_shared)

        @pl.when(ahead & (y == 0))
        def _():
            r_buf[x, half] = times(times(s_buf[3, half], s_buf[2]), z_buf[...])

        @pl.when(ahead & (y == 1))
        def _():
            r_buf[x, half] = times(s_buf[3, half], z_buf[...])

        @pl.when(ahead & (y == 2))
        def _():
            r_buf[x, half] = times(n_buf[...], s_buf[0])

        @pl.when(ahead & (y == 3))
        def _():
            r_buf[x, half] = times(times(n_buf[...], s_buf[1]), s_buf[0])

        x_copy, x_share, x_shared = gather(r_buf, xs_sem, xr_sem, xd_sem, xe_sem, right_x, left_x)

        to_right = x < 3
        first = x == 0
        last = x == 3
        x_out = []

        def when_start(cond, copy):
            @pl.when(cond)
            def _():
                copy.start()
            x_out.append((cond, copy))

        def when_recv(cond, copy):
            @pl.when(cond)
            def _():
                copy.wait_recv()

        when_start(to_right, x_copy(x, 0, right_x, 0))
        when_start(x < 2, x_copy(x, 1, left_x, 3))
        when_start(to_right, x_copy(x, 1, right_x, 1))
        when_start(first, x_copy(x, 0, left_x, 2))
        pl.when(y == 1)(opposite_shared)

        @pl.when(y == 1)
        def _():
            l_buf[...] = s_buf[0]

        @pl.when(y >= 2)
        def _():
            l_buf[...] = times(s_buf[1], s_buf[0])

        @pl.when((c == 1) & (y == 0))
        def _():
            l_buf[...] = ao[...]

        x_sh = {}

        def share_r(cond, place, k, n):
            copy = x_share(place, k, n)
            when_start(cond, copy)
            x_sh[n] = (cond, x_shared(place, k, n))

        from_left = x > 0
        opposite = x > 1
        when_recv(from_left, x_copy(xl, 0, left_x, 0))
        for m in range(2):
            when_start((x == 1) | (x == 2), x_copy(xl, m, right_x, 4 + m))
        when_recv(first | last, x_copy(xr, 1, right_x, 3))
        for m in range(2):
            when_start(first | last, x_copy(xr, 2 + m, left_x, 6 + m))
        share_r(from_left, xl, 0, 0)
        share_r(last, xr, 1, 3)

        @pl.when(y == 3)
        def _():
            l_buf[...] = times(s_buf[2], l_buf[...])

        @pl.when((c == 1) & (y > 0))
        def _():
            l_buf[...] = times(ao[...], l_buf[...])

        when_recv(from_left, x_copy(xl, 1, left_x, 1))
        share_r(from_left, xl, 1, 1)
        when_recv(last, x_copy(xr, 0, left_x, 2))
        share_r(last, xr, 0, 2)

        rest = h_buf.at[pl.ds(0, (NZ - 1) * HB)]
        remote(rest, rest, hs_sem.at[0], hr_sem.at[0], sib).wait_recv()
        inner = (y > 0) | (c > 0)

        @pl.when(jnp.logical_not(inner))
        def _():
            z_buf[...] = h_buf[...]

        @pl.when(inner)
        def _():
            z_buf[...] = times(l_buf[...], times(h_buf[...], l_buf[...]), TN)

        z_copy = remote(z_buf, zo_buf, zz_sem.at[0], zz_sem.at[1], sib)
        z_copy.start()

        part = z
        place = lax.broadcasted_iota(jnp.int32, (WIDE, D), 0)
        column = lax.broadcasted_iota(jnp.int32, (WIDE, D), 1)
        within = place & (PIECE - 1)
        wanted = part * (8 * ROWS) + (c * 4 + (place >> 4)) * ROWS + within
        u_buf[...] = jnp.where((within < ROWS) & (column == wanted), 1.0, 0.0).astype(F32)
        for n in (0, 3, 1, 2):
            when_recv(*x_sh[n])

        @pl.when((x == 1) | last)
        def _():
            u_buf[...] = times(u_buf[...], r_buf[0], NT)

        for k, n in ((0, 4), (2, 6), (1, 5), (3, 7)):
            when_recv(opposite, x_copy(xo, k, left_x, n))
            share_r(opposite, xo, k, n)
        for n in (4, 6, 5, 7):
            when_recv(*x_sh[n])

        @pl.when(x == 2)
        def _():
            u_buf[...] = times(u_buf[...], r_buf[0], NT)
        for k in (1, 2):
            @pl.when(x > k)
            def _(k=k):
                u_buf[...] = times(u_buf[...], r_buf[k], NT)
        z_copy.wait_recv()
        u_buf[...] = times(u_buf[...], z_buf[...] + zo_buf[...])

        t_out = []
        for q in range(4):
            yt, ct = c * 2 + q // 2, q % 2
            mine = (y == yt) & (c == ct)
            copy = remote(u_buf.at[pl.ds(q * PIECE, PIECE)], t_buf.at[y], ts_sem.at[q], tr_sem.at[y],
                          (x, yt, ct, z))

            @pl.when(mine)
            def _(q=q):
                t_buf[y] = u_buf[pl.ds(q * PIECE, PIECE)]

            @pl.when(jnp.logical_not(mine))
            def _(copy=copy):
                copy.start()
            t_out.append((jnp.logical_not(mine), copy))

        @pl.when(x >= 2)
        def _():
            l_buf[...] = times(r_buf[1], r_buf[0])

        @pl.when(x == 3)
        def _():
            l_buf[...] = times(r_buf[2], l_buf[...])
        holder = c == lax.div(y, 2)
        for k in range(NY):
            @pl.when(jnp.logical_not(holder & (y == k)))
            def _(k=k):
                remote(t_buf.at[k], t_buf.at[k], ts_sem.at[0], tr_sem.at[k], sib).wait_recv()
        v_buf[...] = (t_buf[0] + t_buf[1]) + (t_buf[2] + t_buf[3])

        @pl.when(x == 1)
        def _():
            v_buf[...] = times(v_buf[...], r_buf[0])

        @pl.when(x >= 2)
        def _():
            v_buf[...] = times(v_buf[...], l_buf[...])

        g_copy = remote(v_buf, g_buf.at[x], gs_sem.at[0], gr_sem.at[x], (z, y, c, z))

        @pl.when(jnp.logical_not(owner))
        def _():
            g_copy.start()

        @pl.when(owner)
        def _():
            total = v_buf[...]
            for k in (1, 3, 2):
                k = lax.rem(x + k, NX)
                remote(g_buf.at[k], g_buf.at[k], gs_sem.at[0], gr_sem.at[k], sib).wait_recv()
            for k in (1, 3, 2):
                total = total + g_buf[lax.rem(x + k, NX)]
            e_buf[0] = total[:ROWS]
            for k in (7, 8, 6, 9, 5, 10, 4, 11, 3, 12, 2, 13, 1, 14, 0):
                e_out[k].start()
            o_ref[...] = total[:ROWS]

        @pl.when(jnp.logical_not(owner))
        def _():
            g_copy.wait_send()

        @pl.when(c == 0)
        def _():
            for copy in a_up:
                copy.wait_send()

        @pl.when(c == 1)
        def _():
            for copy in a_down:
                copy.wait_send()
        z_copy.wait_send()
        for copy in y_out:
            copy.wait_send()
        for copy, _ in y_sh.values():
            copy.wait_send()
        for cond, copy in x_out + t_out:
            pl.when(cond)(copy.wait_send)

    @pl.when(worker)
    def _():
        work()

    @pl.when(jnp.logical_not(worker))
    def _():
        send_rows()

    @pl.when(owner)
    def _():
        for copy in e_out:
            copy.wait_send()

    @pl.when(jnp.logical_not(owner))
    def _():
        e_out[0].wait_recv()
        o_ref[...] = e_buf[1]

    for k, copy in enumerate(h_out):
        pl.when(z != k)(copy.wait_send)


def body(propagators, perturbation):
    full = pltpu.VMEM((D, D), F32)
    dma = pltpu.SemaphoreType.DMA
    return pl.pallas_call(
        kernel,
        out_shape=jax.ShapeDtypeStruct((ROWS, D), F32),
        in_specs=[pl.BlockSpec(memory_space=pltpu.HBM)] * 2,
        out_specs=pl.BlockSpec(memory_space=pltpu.VMEM),
        scratch_shapes=[
            full, full,
            pltpu.VMEM((NY, D, D), F32),
            pltpu.VMEM((NX, D, D), F32),
            full, full, full, full,
            pltpu.VMEM((WIDE, D), F32),
            pltpu.VMEM((NY, PIECE, D), F32),
            pltpu.VMEM((PIECE, D), F32),
            pltpu.VMEM((NX, PIECE, D), F32),
            pltpu.VMEM((HALF, D), F32),
            pltpu.VMEM((2, ROWS, D), F32),
            dma((2,)), dma((4,)),
            dma((8,)), dma((8,)), dma((10,)), dma((10,)),
            dma((8,)), dma((8,)), dma((8,)), dma((8,)),
            dma((NW,)), dma((1,)), dma((2,)),
            dma((4,)), dma((4,)),
            dma((1,)), dma((4,)),
            dma((NZ - 1,)), dma((1,)),
        ],
        compiler_params=pltpu.CompilerParams(
            collective_id=0, has_side_effects=True, vmem_limit_bytes=55192 * 1024),
        name="floquet",
    )(propagators, perturbation)


def solution(mesh):
    split = Mesh(mesh.devices.reshape(NX, NY, 2, NZ), AXES)
    tm = ("x", "y", "c")
    return jax.shard_map(
        body,
        mesh=split,
        in_specs=(P(tm, None, None), P(tm, "z", None)),
        out_specs=P(tm, None),
        check_vma=False,
    )
```

time: 198 us -> 51.5 us (0.26)
  the two profiles are of different devices: /device:TPU:8 before, /device:TPU:6 now
where the time goes in v3:
time: 51.5 us; the launch traced here: 51.3 us
  Pallas kernels  50.7 us (98%)
  local copies, waits for them, and re-layouts  0.61 us (1%)
    pallas_call x1, Pallas kernels, body(): pl.pallas_call(kernel, out_shape=jax.ShapeDtypeStruct((ROWS, D), F32), in...  50.7 us

profile of v3, /device:TPU:6, one launch (start us, length us, event | category | flops | bytes accessed | tf_op | source)
XLA Modules:
  0.0 51.3 jit_solution(5990135946748234334)
XLA Ops:
  0.0 50.7 %floquet.1 = f32[12,384]{1,0:T(8,128)S(1)} custom-call(f32[1,384,384]{2,1,0:T(8,128)} %a_hbm.1, f32[1,24,384]{2,1,0:T(8,128)} %h_hbm.1), custom_call_target="tpu_custom_call" | custom-call | tf_op jit(solution)/shard_map/floquet/pallas_call | solution.py:446
  50.7 0.6 %copy.4 = f32[12,384]{1,0:T(8,128)} copy(f32[12,384]{1,0:T(8,128)S(1)} %floquet.1) | data formatting | bytes 36864

commit v4 on v3

--- a/solution.py
+++ b/solution.py
@@ -17,10 +17,13 @@
 NX = 4
 NY = 4
 NZ = 16
-NW = 4
+FIRST = 1
+NW = 2
 HB = D // NZ
 ROWS = D // 32
-PIECE = 16
+UNIT = 16
+SUB = NX // NW
+PIECE = SUB * UNIT
 WIDE = 4 * PIECE
 NN = ((1,), (0,))
 NT = ((1,), (1,))
@@ -47,11 +50,12 @@
 
 
 def kernel(a_hbm, h_hbm, o_ref, av, ao, s_buf, r_buf, h_buf, l_buf, z_buf, zo_buf, u_buf, t_buf, v_buf, g_buf, n_buf,
-           e_buf, in_sem, a_sem, ys_sem, yr_sem, yd_sem, ye_sem, xs_sem, xr_sem, xd_sem, xe_sem,
+           e_buf, w_buf, f_buf, in_sem, a_sem, ys_sem, yr_sem, yd_sem, ye_sem, xs_sem, xr_sem, xd_sem, xe_sem,
            hs_sem, hr_sem, zz_sem, ts_sem, tr_sem, gs_sem, gr_sem, es_sem, er_sem):
     x, y, c, z = (lax.axis_index(a) for a in AXES)
-    worker = z < NW
-    owner = z == x
+    worker = (z >= FIRST) & (z < FIRST + NW)
+    owner = z == FIRST + lax.div(x, SUB)
+    lot = (z - FIRST) * SUB
     here = pl.ds(z * HB, HB)
     a_load = pltpu.make_async_copy(a_hbm.at[0], av, in_sem.at[0])
     h_load = pltpu.make_async_copy(h_hbm.at[0], h_buf.at[here], in_sem.at[1])
@@ -80,12 +84,13 @@
         return pltpu.make_async_remote_copy(
             src_ref=src, dst_ref=dst, send_sem=send, recv_sem=recv, device_id=dev, device_id_type=MESH)
 
-    h_out = [remote(h_buf.at[here], h_buf.at[here], hs_sem.at[k], hr_sem.at[0], (x, y, c, k)) for k in range(NW)]
+    h_out = [remote(h_buf.at[here], h_buf.at[here], hs_sem.at[k], hr_sem.at[0], (x, y, c, FIRST + k))
+             for k in range(NW)]
 
     def send_rows():
         h_load.wait()
         for k, copy in enumerate(h_out):
-            pl.when(z != k)(copy.start)
+            pl.when(z != FIRST + k)(copy.start)
 
     e_out = [remote(e_buf.at[0], e_buf.at[1], es_sem.at[k], er_sem.at[0], dev)
              for k, dev in enumerate(others)]
@@ -265,6 +270,14 @@
         def _():
             l_buf[...] = ao[...]
 
+        @pl.when(y == 3)
+        def _():
+            l_buf[...] = times(s_buf[2], l_buf[...])
+
+        @pl.when((c == 1) & (y > 0))
+        def _():
+            l_buf[...] = times(ao[...], l_buf[...])
+
         x_sh = {}
 
         def share_r(cond, place, k, n):
@@ -283,39 +296,31 @@
         share_r(from_left, xl, 0, 0)
         share_r(last, xr, 1, 3)
 
-        @pl.when(y == 3)
-        def _():
-            l_buf[...] = times(s_buf[2], l_buf[...])
-
-        @pl.when((c == 1) & (y > 0))
-        def _():
-            l_buf[...] = times(ao[...], l_buf[...])
+        rest = h_buf.at[pl.ds(0, (NZ - 1) * HB)]
+        remote(rest, rest, hs_sem.at[0], hr_sem.at[0], sib).wait_recv()
+        inner = (y > 0) | (c > 0)
+
+        @pl.when(jnp.logical_not(inner))
+        def _():
+            z_buf[...] = h_buf[...]
+
+        @pl.when(inner)
+        def _():
+            z_buf[...] = times(l_buf[...], times(h_buf[...], l_buf[...]), TN)
+
+        z_copy = remote(z_buf, zo_buf, zz_sem.at[0], zz_sem.at[1], sib)
+        z_copy.start()
 
         when_recv(from_left, x_copy(xl, 1, left_x, 1))
         share_r(from_left, xl, 1, 1)
         when_recv(last, x_copy(xr, 0, left_x, 2))
         share_r(last, xr, 0, 2)
 
-        rest = h_buf.at[pl.ds(0, (NZ - 1) * HB)]
-        remote(rest, rest, hs_sem.at[0], hr_sem.at[0], sib).wait_recv()
-        inner = (y > 0) | (c > 0)
-
-        @pl.when(jnp.logical_not(inner))
-        def _():
-            z_buf[...] = h_buf[...]
-
-        @pl.when(inner)
-        def _():
-            z_buf[...] = times(l_buf[...], times(h_buf[...], l_buf[...]), TN)
-
-        z_copy = remote(z_buf, zo_buf, zz_sem.at[0], zz_sem.at[1], sib)
-        z_copy.start()
-
-        part = z
         place = lax.broadcasted_iota(jnp.int32, (WIDE, D), 0)
         column = lax.broadcasted_iota(jnp.int32, (WIDE, D), 1)
-        within = place & (PIECE - 1)
-        wanted = part * (8 * ROWS) + (c * 4 + (place >> 4)) * ROWS + within
+        within = lax.rem(place, UNIT)
+        block = lot + lax.rem(lax.div(place, UNIT), SUB)
+        wanted = block * (8 * ROWS) + (lax.div(place, PIECE) * 2 + c) * ROWS + within
         u_buf[...] = jnp.where((within < ROWS) & (column == wanted), 1.0, 0.0).astype(F32)
         for n in (0, 3, 1, 2):
             when_recv(*x_sh[n])
@@ -327,35 +332,49 @@
         for k, n in ((0, 4), (2, 6), (1, 5), (3, 7)):
             when_recv(opposite, x_copy(xo, k, left_x, n))
             share_r(opposite, xo, k, n)
+
+        z_copy.wait_recv()
+        z_copy.wait_send()
+        z_buf[...] = z_buf[...] + zo_buf[...]
+
+        @pl.when(x == 2)
+        def _():
+            z_buf[...] = times(r_buf[1], z_buf[...], TN)
+
+        @pl.when(x == 3)
+        def _():
+            z_buf[...] = times(r_buf[2], z_buf[...], TN)
         for n in (4, 6, 5, 7):
             when_recv(*x_sh[n])
 
         @pl.when(x == 2)
         def _():
             u_buf[...] = times(u_buf[...], r_buf[0], NT)
-        for k in (1, 2):
-            @pl.when(x > k)
-            def _(k=k):
-                u_buf[...] = times(u_buf[...], r_buf[k], NT)
-        z_copy.wait_recv()
-        u_buf[...] = times(u_buf[...], z_buf[...] + zo_buf[...])
+
+        @pl.when(x == 3)
+        def _():
+            u_buf[...] = times(u_buf[...], r_buf[1], NT)
+        u_buf[...] = times(u_buf[...], z_buf[...])
 
         t_out = []
         for q in range(4):
-            yt, ct = c * 2 + q // 2, q % 2
-            mine = (y == yt) & (c == ct)
-            copy = remote(u_buf.at[pl.ds(q * PIECE, PIECE)], t_buf.at[y], ts_sem.at[q], tr_sem.at[y],
-                          (x, yt, ct, z))
+            for k in range(SUB):
+                w_buf[q, k] = u_buf[pl.ds(q * PIECE + k * UNIT, ROWS)]
+        for q in range(4):
+            mine = y == q
+            copy = remote(w_buf.at[q], t_buf.at[y], ts_sem.at[q], tr_sem.at[y], (x, q, c, z))
 
             @pl.when(mine)
             def _(q=q):
-                t_buf[y] = u_buf[pl.ds(q * PIECE, PIECE)]
+                t_buf[y] = w_buf[q]
 
             @pl.when(jnp.logical_not(mine))
             def _(copy=copy):
                 copy.start()
             t_out.append((jnp.logical_not(mine), copy))
 
+        v_buf[...] = jnp.zeros((PIECE, D), F32)
+
         @pl.when(x >= 2)
         def _():
             l_buf[...] = times(r_buf[1], r_buf[0])
@@ -363,43 +382,48 @@
         @pl.when(x == 3)
         def _():
             l_buf[...] = times(r_buf[2], l_buf[...])
-        holder = c == lax.div(y, 2)
         for k in range(NY):
-            @pl.when(jnp.logical_not(holder & (y == k)))
+            @pl.when(y != k)
             def _(k=k):
                 remote(t_buf.at[k], t_buf.at[k], ts_sem.at[0], tr_sem.at[k], sib).wait_recv()
-        v_buf[...] = (t_buf[0] + t_buf[1]) + (t_buf[2] + t_buf[3])
+        for k in range(SUB):
+            v_buf[pl.ds(k * UNIT, ROWS)] = (t_buf[0, k] + t_buf[1, k]) + (t_buf[2, k] + t_buf[3, k])
+        value = v_buf[...]
+
+        def place_pieces(value):
+            for k in range(SUB):
+                f_buf[k] = value[k * UNIT:k * UNIT + ROWS]
+
+        @pl.when(x == 0)
+        def _():
+            place_pieces(value)
 
         @pl.when(x == 1)
         def _():
-            v_buf[...] = times(v_buf[...], r_buf[0])
+            place_pieces(times(value, r_buf[0]))
 
         @pl.when(x >= 2)
         def _():
-            v_buf[...] = times(v_buf[...], l_buf[...])
-
-        g_copy = remote(v_buf, g_buf.at[x], gs_sem.at[0], gr_sem.at[x], (z, y, c, z))
-
-        @pl.when(jnp.logical_not(owner))
-        def _():
-            g_copy.start()
+            place_pieces(times(value, l_buf[...]))
+
+        for k in range(SUB):
+            there = lot + k
+            copy = remote(f_buf.at[k], g_buf.at[x], gs_sem.at[k], gr_sem.at[x], (there, y, c, z))
+            pl.when(x != there)(copy.start)
+            t_out.append((x != there, copy))
 
         @pl.when(owner)
         def _():
-            total = v_buf[...]
+            total = f_buf[x - lot]
             for k in (1, 3, 2):
                 k = lax.rem(x + k, NX)
                 remote(g_buf.at[k], g_buf.at[k], gs_sem.at[0], gr_sem.at[k], sib).wait_recv()
             for k in (1, 3, 2):
                 total = total + g_buf[lax.rem(x + k, NX)]
-            e_buf[0] = total[:ROWS]
+            e_buf[0] = total
             for k in (7, 8, 6, 9, 5, 10, 4, 11, 3, 12, 2, 13, 1, 14, 0):
                 e_out[k].start()
-            o_ref[...] = total[:ROWS]
-
-        @pl.when(jnp.logical_not(owner))
-        def _():
-            g_copy.wait_send()
+            o_ref[...] = total
 
         @pl.when(c == 0)
         def _():
@@ -410,7 +434,6 @@
         def _():
             for copy in a_down:
                 copy.wait_send()
-        z_copy.wait_send()
         for copy in y_out:
             copy.wait_send()
         for copy, _ in y_sh.values():
@@ -437,7 +460,7 @@
         o_ref[...] = e_buf[1]
 
     for k, copy in enumerate(h_out):
-        pl.when(z != k)(copy.wait_send)
+        pl.when(z != FIRST + k)(copy.wait_send)
 
 
 def body(propagators, perturbation):
@@ -454,17 +477,19 @@
             pltpu.VMEM((NX, D, D), F32),
             full, full, full, full,
             pltpu.VMEM((WIDE, D), F32),
-            pltpu.VMEM((NY, PIECE, D), F32),
+            pltpu.VMEM((NY, SUB, ROWS, D), F32),
             pltpu.VMEM((PIECE, D), F32),
-            pltpu.VMEM((NX, PIECE, D), F32),
+            pltpu.VMEM((NX, ROWS, D), F32),
             pltpu.VMEM((HALF, D), F32),
             pltpu.VMEM((2, ROWS, D), F32),
+            pltpu.VMEM((4, SUB, ROWS, D), F32),
+            pltpu.VMEM((SUB, ROWS, D), F32),
             dma((2,)), dma((4,)),
             dma((8,)), dma((8,)), dma((10,)), dma((10,)),
             dma((8,)), dma((8,)), dma((8,)), dma((8,)),
             dma((NW,)), dma((1,)), dma((2,)),
             dma((4,)), dma((4,)),
-            dma((1,)), dma((4,)),
+            dma((SUB,)), dma((4,)),
             dma((NZ - 1,)), dma((1,)),
         ],
         compiler_params=pltpu.CompilerParams(

time: 51.5 us -> 49.5 us (0.961)
  the two profiles are of different devices: /device:TPU:6 before, /device:TPU:1 now
where the time goes in v4:
time: 49.5 us; the launch traced here: 49.3 us
  Pallas kernels  48.7 us (98%)
  local copies, waits for them, and re-layouts  0.61 us (1%)
    pallas_call x1, Pallas kernels, body(): pl.pallas_call(kernel, out_shape=jax.ShapeDtypeStruct((ROWS, D), F32), in...  48.7 us

profile of v4, /device:TPU:1, one launch (start us, length us, event | category | flops | bytes accessed | tf_op | source)
XLA Modules:
  0.0 49.3 jit_solution(18302456648043412114)
XLA Ops:
  0.0 48.7 %floquet.1 = f32[12,384]{1,0:T(8,128)S(1)} custom-call(f32[1,384,384]{2,1,0:T(8,128)} %a_hbm.1, f32[1,24,384]{2,1,0:T(8,128)} %h_hbm.1), custom_call_target="tpu_custom_call" | custom-call | tf_op jit(solution)/shard_map/floquet/pallas_call | solution.py:469
  48.7 0.6 %copy.4 = f32[12,384]{1,0:T(8,128)} copy(f32[12,384]{1,0:T(8,128)S(1)} %floquet.1) | data formatting | bytes 36864

commit v5 on v4

--- a/solution.py
+++ b/solution.py
@@ -421,7 +421,7 @@
             for k in (1, 3, 2):
                 total = total + g_buf[lax.rem(x + k, NX)]
             e_buf[0] = total
-            for k in (7, 8, 6, 9, 5, 10, 4, 11, 3, 12, 2, 13, 1, 14, 0):
+            for k in (14, 0, 13, 1, 2, 3, 4, 5, 12, 11, 10, 6, 7, 8, 9):
                 e_out[k].start()
             o_ref[...] = total
 

time: 49.5 us -> 47.6 us (0.962); the launches traced: 49.3 us -> 46.7 us
  Pallas kernels: 48.7 us -> 46.1 us
    pallas_call x1, Pallas kernels: 48.7 us -> 46.1 us  [body(): pl.pallas_call(kernel, out_shape=jax.ShapeDtypeStruct((ROWS, D), F32), in...]
where the time goes in v5:
time: 47.6 us; the launch traced here: 46.7 us
  Pallas kernels  46.1 us (97%)
  local copies, waits for them, and re-layouts  0.61 us (1%)
    pallas_call x1, Pallas kernels, body(): pl.pallas_call(kernel, out_shape=jax.ShapeDtypeStruct((ROWS, D), F32), in...  46.1 us

profile of v5, /device:TPU:1, one launch (start us, length us, event | category | flops | bytes accessed | tf_op | source)
XLA Modules:
  0.0 46.7 jit_solution(3934809977800661965)
XLA Ops:
  0.0 46.1 %floquet.1 = f32[12,384]{1,0:T(8,128)S(1)} custom-call(f32[1,384,384]{2,1,0:T(8,128)} %a_hbm.1, f32[1,24,384]{2,1,0:T(8,128)} %h_hbm.1), custom_call_target="tpu_custom_call" | custom-call | tf_op jit(solution)/shard_map/floquet/pallas_call | solution.py:469
  46.1 0.6 %copy.4 = f32[12,384]{1,0:T(8,128)} copy(f32[12,384]{1,0:T(8,128)S(1)} %floquet.1) | data formatting | bytes 36864

commit v6 on v5

--- a/solution.py
+++ b/solution.py
@@ -104,7 +104,8 @@
             return [remote(av.at[w], ao.at[w], a_sem.at[k], a_sem.at[2 + k], sib) for k, w in enumerate(where)]
 
         a_down = a_copies(low0, low1)
-        a_up = a_copies(low, high)
+        top, bottom = pl.ds(0, 256), pl.ds(256, D - 256)
+        a_up = a_copies(top, bottom)
         a_load.wait()
 
         @pl.when(c == 0)
@@ -161,9 +162,10 @@
 
         @pl.when(c == 1)
         def _():
-            for copy in a_up:
-                copy.wait_recv()
-            s_buf[y, high] = times(av[high], ao[...])
+            a_up[0].wait_recv()
+            value = times(av[high, top], ao[top])
+            a_up[1].wait_recv()
+            s_buf[y, high] = value + times(av[high, bottom], ao[bottom])
             y_out[0].start()
 
         for copy in y_out[1:]:
@@ -421,7 +423,7 @@
             for k in (1, 3, 2):
                 total = total + g_buf[lax.rem(x + k, NX)]
             e_buf[0] = total
-            for k in (14, 0, 13, 1, 2, 3, 4, 5, 12, 11, 10, 6, 7, 8, 9):
+            for k in (14, 13, 0, 1, 2, 3, 4, 12, 5, 11, 10, 6, 7, 8, 9):
                 e_out[k].start()
             o_ref[...] = total
 

time: 47.6 us -> 47.7 us (level)
  no operation moved by 1% of the time
where the time goes in v6:
time: 47.7 us; the launch traced here: 46.8 us
  Pallas kernels  46.1 us (97%)
  local copies, waits for them, and re-layouts  0.61 us (1%)
    pallas_call x1, Pallas kernels, body(): pl.pallas_call(kernel, out_shape=jax.ShapeDtypeStruct((ROWS, D), F32), in...  46.1 us

profile of v6, /device:TPU:1, one launch (start us, length us, event | category | flops | bytes accessed | tf_op | source)
XLA Modules:
  0.0 46.8 jit_solution(185451909545755884)
XLA Ops:
  0.0 46.1 %floquet.1 = f32[12,384]{1,0:T(8,128)S(1)} custom-call(f32[1,384,384]{2,1,0:T(8,128)} %a_hbm.1, f32[1,24,384]{2,1,0:T(8,128)} %h_hbm.1), custom_call_target="tpu_custom_call" | custom-call | tf_op jit(solution)/shard_map/floquet/pallas_call | solution.py:471
  46.1 0.6 %copy.4 = f32[12,384]{1,0:T(8,128)} copy(f32[12,384]{1,0:T(8,128)S(1)} %floquet.1) | data formatting | bytes 36864

commit v7 on v6

--- a/solution.py
+++ b/solution.py
@@ -356,13 +356,13 @@
         @pl.when(x == 3)
         def _():
             u_buf[...] = times(u_buf[...], r_buf[1], NT)
-        u_buf[...] = times(u_buf[...], z_buf[...])
 
         t_out = []
         for q in range(4):
-            for k in range(SUB):
-                w_buf[q, k] = u_buf[pl.ds(q * PIECE + k * UNIT, ROWS)]
-        for q in range(4):
+            if q % 2 == 0:
+                value = times(u_buf[pl.ds(q * PIECE, 2 * PIECE)], z_buf[...])
+                for k in range(2 * SUB):
+                    w_buf[q + k // SUB, k % SUB] = value[k * UNIT:k * UNIT + ROWS]
             mine = y == q
             copy = remote(w_buf.at[q], t_buf.at[y], ts_sem.at[q], tr_sem.at[y], (x, q, c, z))
 

time: 47.7 us -> 47.6 us (level)
  no operation moved by 1% of the time
where the time goes in v7:
time: 47.6 us; the launch traced here: 46.7 us
  Pallas kernels  46 us (97%)
  local copies, waits for them, and re-layouts  0.61 us (1%)
    pallas_call x1, Pallas kernels, body(): pl.pallas_call(kernel, out_shape=jax.ShapeDtypeStruct((ROWS, D), F32), in...  46 us

profile of v7, /device:TPU:1, one launch (start us, length us, event | category | flops | bytes accessed | tf_op | source)
XLA Modules:
  0.0 46.7 jit_solution(14101493488350003557)
XLA Ops:
  0.0 46.0 %floquet.1 = f32[12,384]{1,0:T(8,128)S(1)} custom-call(f32[1,384,384]{2,1,0:T(8,128)} %a_hbm.1, f32[1,24,384]{2,1,0:T(8,128)} %h_hbm.1), custom_call_target="tpu_custom_call" | custom-call | tf_op jit(solution)/shard_map/floquet/pallas_call | solution.py:471
  46.1 0.6 %copy.4 = f32[12,384]{1,0:T(8,128)} copy(f32[12,384]{1,0:T(8,128)S(1)} %floquet.1) | data formatting | bytes 36864
